TPU v7x, 32 devices: a whole 2x2x4 slice. The times are simulated.
32 devices in a mesh: node: 8 (over z, x), feat: 4 (over y, core).
Axes of the slice: x: 2, y: 2, z: 4, core: 2. Of those that a mesh axis runs over, the one named last changes fastest.
Arguments:
- out_grad: bfloat16 [256, 65536], P('feat', 'node'), may hold values from -6 to 6
- pre_act: bfloat16 [256, 65536], P('feat', 'node'), may hold values from -6 to 6
- in_act: bfloat16 [256, 65536], P(None, ('node', 'feat')), may hold values from -6 to 6
- weight: bfloat16 [256, 256], replicated, may hold values from -0.375 to 0.375
- tiles: bfloat16 [512, 24, 128, 128], P('node'), may hold values from -0.4375 to 0.4375
- indices: int32 [512, 24], P('node'), may hold values from 0 to 511, as said below
- counts: int32 [512], P('node'), may hold values from 1 to 24, as said below
Outputs:
- in_grad: bfloat16 [256, 65536], P(None, ('node', 'feat'))
- weight_grad: float32 [256, 256], replicated
Inputs may be any that keep to these rules, and one draw needn't show every extreme that they name: `indices`: the 24 column blocks named by one row block are distinct; slots at or after the row block's count are ignored. Each node device has a cap between 2 and 24, and its row blocks' counts are at most that cap, except for one row block in the whole graph whose count is 24.
All inputs are finite; a program needn't handle non-finite values.
Results may differ from a plain program's by a relative error of at most 0.012.
Values may be sent and summed in bfloat16 or wider, within the bound.
A program may use at most 192 MiB of HBM per device.

v0:
```python
import jax
import jax.numpy as jnp
from jax import lax
from jax.sharding import PartitionSpec as P


def per_device(out_grad, pre_act, in_act, weight, tiles, indices, counts):
    grad_pre = jnp.where(pre_act > 0, out_grad, jnp.zeros_like(out_grad))
    whole = lax.all_gather(grad_pre, "node", axis=1, tiled=True)
    feat_rows = whole.shape[0]
    block_size = tiles.shape[2]
    slot_count = tiles.shape[1]
    local_rows = grad_pre.shape[1]
    blocks = whole.reshape(feat_rows, whole.shape[1] // block_size, block_size)
    picked = jnp.take(blocks, indices, axis=1)
    slots = jnp.arange(slot_count, dtype=jnp.int32)
    live = (slots[None, :] < counts[:, None]).astype(jnp.bfloat16)
    picked = picked * live[None, :, :, None]
    summed = jnp.einsum("frkc,rkic->fri", picked, tiles, preferred_element_type=jnp.float32)
    aggregated = summed.reshape(feat_rows, local_rows).astype(jnp.bfloat16)
    scale = float(whole.shape[1]) ** (-0.5)
    node_rows = lax.all_to_all(aggregated, "feat", split_axis=1, concat_axis=0, tiled=True)
    in_grad = jnp.dot(weight, node_rows, preferred_element_type=jnp.float32).astype(jnp.bfloat16)
    group_acts = lax.all_gather(in_act, "feat", axis=1, tiled=True)
    column_part = (
        lax.dot_general(
            group_acts, aggregated, (((1,), (1,)), ((), ())), preferred_element_type=jnp.float32
        )
        * scale
    )
    column_part = lax.psum(column_part.astype(jnp.bfloat16), "node").astype(jnp.float32)
    weight_grad = lax.all_gather(
        column_part.astype(jnp.bfloat16), "feat", axis=1, tiled=True
    ).astype(column_part.dtype)
    return (in_grad, weight_grad)


def solution(mesh):
    in_specs = (
        P("feat", "node"),
        P("feat", "node"),
        P(None, ("node", "feat")),
        P(),
        P("node", None, None, None),
        P("node", None),
        P("node"),
    )
    out_specs = (P(None, ("node", "feat")), P())
    return jax.shard_map(
        per_device, mesh=mesh, in_specs=in_specs, out_specs=out_specs, check_vma=False
    )
```

profile of v0, /device:TPU:0, one launch (start us, length us, event | category | flops | bytes accessed | tf_op | source)
XLA Modules:
  0.0 272.0 jit_solution(17002543803005956684)
XLA Ops:
  7.2 0.0 copy-start
  7.2 0.0 all-gather.3.cloned.1.call-start
  7.2 2.7 compare_select_fusion
  9.9 0.0 all-gather.3.cloned.1.call-update
  9.9 0.0 all-gather.5.cloned.1.call-start
  10.0 0.7 all-gather.5.cloned.1.call-update
  10.7 0.7 compare_select_fusion.1
  11.4 0.1 copy.29
  11.5 0.1 reshape.44
  11.5 0.7 compare_and_fusion
  12.3 0.1 copy.28
  12.4 0.7 fusion.14
  13.1 125.3 %all-gather.3.cloned.1.call-done = bf16[64,65536]{1,0:T(8,128)(2,1)} async-done(((bf16[64,8192]{1,0:T(8,128)(2,1)}), bf16[64,65536]{1,0:T(8,128)(2,1)}) %all-gather.3.cloned.1.call-update) | async-done | bytes 8388624 | tf_op jit(solution)/shard_map/all_gather | solution.py:9
  138.4 9.7 %copy_bitcast_fusion = bf16[64,512,128]{2,0,1:T(8,128)(2,1)} fusion(bf16[64,65536]{1,0:T(8,128)(2,1)} %all-gather.3.cloned.1.call-done), kind=kLoop, calls=%fused_computation.8 | loop fusion | bytes 16777216 | tf_op jit(solution)/shard_map/reshape | solution.py:14
  148.1 37.1 %gather_fusion = bf16[1536,64,128]{2,1,0:T(8,128)(2,1)} fusion(bf16[64,512,128]{2,0,1:T(8,128)(2,1)} %copy_bitcast_fusion, s32[2048]{0:T(1024)S(1)} %pad_clamp_fusion), kind=kCustom, calls=%fused_computation | custom fusion | bytes 50337792 | tf_op jit(solution)/shard_map/jit(_take)/gather | solution.py:15
  185.2 27.3 %bitcast_convert_fusion = bf16[64,64,128]{2,1,0:T(8,128)(2,1)S(1)} fusion(bf16[64,24,128,128]{3,2,1,0:T(8,128)(2,1)} %param.11, bf16[64,24,64,128]{3,2,1,0:T(8,128)(2,1)} %bitcast.33, pred[64,24]{1,0:T(8,128)(4,1)S(1)} %copy.28, bf16[64,24]{1,0:T(8,128)(2,1)S(1)} %fusion.14), kind=kOutput, calls=%fused_computation.11 | convolution fusion | flops 3246915584 | bytes 76550656 | tf_op jit(solution)/shard_map/frkc,rkic->fri/dot_general | solution.py:19
  212.5 0.7 copy.31
  213.2 0.3 convert_element_type.41
  213.5 1.5 copy.32
  215.1 3.7 %all-to-all-start = ((bf16[64,4,2048]{2,0,1:T(8,128)(2,1)}), bf16[64,4,2048]{2,0,1:T(8,128)(2,1)S(1)}, u32[]{:S(2)}, u32[]{:S(2)}) async-start(bf16[64,4,2048]{2,0,1:T(8,128)(2,1)} %copy.32), calls=%async_computation | async-start | bytes 2097152 | tf_op jit(solution)/shard_map/all_to_all | solution.py:22
  218.8 0.0 all-gather.5.cloned.1.call-done
  218.8 3.6 %fusion.11 = bf16[256,64]{0,1:T(8,128)(2,1)S(1)} fusion(bf16[256,8192]{1,0:T(8,128)(2,1)} %all-gather.5.cloned.1.call-done, bf16[64,64,128]{2,1,0:T(8,128)(2,1)S(1)} %bitcast_convert_fusion), kind=kOutput, calls=%fused_computation.15 | convolution fusion | flops 268468224 | bytes 5275648 | tf_op jit(solution)/shard_map/dot_general | solution.py:26
  222.4 34.6 %psum.7 = bf16[256,64]{0,1:T(8,128)(2,1)S(1)} all-reduce(bf16[256,64]{0,1:T(8,128)(2,1)S(1)} %fusion.11), channel_id=1, replica_groups=mesh['node'=8,'feat'=4] {'node'}, use_global_device_ids=true, to_apply=%region_0.1 | all-reduce | flops 16384 | bytes 65536 | tf_op jit(solution)/shard_map/psum | solution.py:31
  257.0 5.4 %all_gather.11 = bf16[256,256]{0,1:T(8,128)(2,1)S(1)} all-gather(bf16[256,64]{0,1:T(8,128)(2,1)S(1)} %psum.7), channel_id=1, replica_groups=mesh['node'=8,'feat'=4] {'feat'}, dimensions={1}, use_global_device_ids=true | all-gather | bytes 163840 | tf_op jit(solution)/shard_map/all_gather | solution.py:32
  262.4 0.8 copy.35
  263.2 0.0 all-to-all-done
  263.2 0.0 copy-done
  263.2 0.5 fusion.7
  263.7 1.4 copy.34
  (1 shorter events, 0.0 us)
Async XLA Ops:
  7.2 256.0 %copy-start = (bf16[256,256]{1,0:T(8,128)(2,1)S(1)}, bf16[256,256]{1,0:T(8,128)(2,1)}, u32[]{:S(2)}) copy-start(bf16[256,256]{1,0:T(8,128)(2,1)} %param.10) | copy-start | bytes 393220
  7.2 131.2 %all-gather.3.cloned.1.call-start = ((), (), s32[]{:S(2)}) async-start(), calls=%async_computation.1 | async-start | bytes 9437184 | tf_op jit(solution)/shard_map/all_gather | solution.py:9
  9.9 208.9 %all-gather.5.cloned.1.call-start = ((), (), s32[]{:S(2)}) async-start(), calls=%async_computation.2 | async-start | bytes 5242880 | tf_op jit(solution)/shard_map/all_gather | solution.py:24
  215.1 48.1 %all-to-all-start = ((bf16[64,4,2048]{2,0,1:T(8,128)(2,1)}), bf16[64,4,2048]{2,0,1:T(8,128)(2,1)S(1)}, u32[]{:S(2)}, u32[]{:S(2)}) async-start(bf16[64,4,2048]{2,0,1:T(8,128)(2,1)} %copy.32), calls=%async_computation | async-start | bytes 2097152 | tf_op jit(solution)/shard_map/all_to_all | solution.py:22
Sparse Core Ops, SparseCore 0:
  10.8 127.5 all-gather.2
  140.0 32.6 all-gather.4
where the time goes:
time: 272 us
  waiting for transfers between devices  126 us (46%)
  local copies, waits for them, and re-layouts  51.8 us (19%)
  blocking collectives  40 us (15%)
  matrix products  31.4 us (12%)
  between operations  14.1 us (5%)
  other arithmetic  4.82 us (2%)
  starting transfers between devices  3.78 us (1%)
    all_gather x1, waiting for transfers between devices, per_device(): whole = lax.all_gather(grad_pre, 'node', axis=1, tiled=True)  125 us
    gather x1, local copies, waits for them, and re-layouts, per_device(): picked = jnp.take(blocks, indices, axis=1)  37.1 us
    psum x1, blocking collectives, per_device(): lax.psum(column_part.astype(jnp.bfloat16), 'node').astype(jnp.float32)  34.6 us
    dot_general x1, matrix products, per_device(): jnp.einsum('frkc,rkic->fri', picked, tiles, preferred_element_type=jnp.fl...  27.3 us
    reshape x1, local copies, waits for them, and re-layouts, per_device(): blocks = whole.reshape(feat_rows, whole.shape[1] // block_size, block_size)  9.71 us
  transfers between devices with their start and end apart: 3, of which 1 were waited for; matrix products, arithmetic and copies ran while one was open for 31% of the time, Pallas kernels for 0%

commit v1 on v0

v1 whole, which is shorter than its diff:
```python
import functools

import jax
import jax.numpy as jnp
from jax import lax
from jax.experimental import pallas as pl
from jax.experimental.pallas import tpu as pltpu
from jax.sharding import PartitionSpec as P

MESH = pl.DeviceIdType.MESH
ROWS = 16
GROUP = 4
DEPTH = 8


def gather_kernel(
    n, m, width, grad_ref, act_ref, in_ref, out_ref, acts_ref,
    own, send_sem, recv_sem, local_sem, in_send, in_recv, in_local,
):
    me = lax.axis_index("node")
    mine = lax.axis_index("feat")
    height = n // width
    z, x = me // width, me % width
    pieces = own.shape[0]
    has = (z > 0, z < height - 1, x > 0, x < width - 1)
    there = (me - width, me + width, me - 1, me + 1)
    over = pieces // 2 if width == 2 and height % 2 == 0 else 0
    mate = z + 1 - 2 * (z % 2)

    barrier = pltpu.get_barrier_semaphore()
    for d in range(4):
        @pl.when(has[d])
        def _():
            pl.semaphore_signal(barrier, inc=1, device_id={"node": there[d]}, device_id_type=MESH)
    for step in range(1, m):
        pl.semaphore_signal(
            barrier, inc=1, device_id={"feat": lax.rem(mine + step, m)}, device_id_type=MESH
        )
    peers = sum(jnp.where(h, 1, 0) for h in has) + (m - 1)
    pl.semaphore_wait(barrier, peers)

    def spread(step):
        return pltpu.make_async_remote_copy(
            src_ref=in_ref,
            dst_ref=acts_ref.at[mine],
            send_sem=in_send.at[step],
            recv_sem=in_recv.at[step],
            device_id={"feat": lax.rem(mine + step, m)},
            device_id_type=MESH,
        )

    def copy(block, c, d, src):
        return pltpu.make_async_remote_copy(
            src_ref=src,
            dst_ref=out_ref.at[block, c],
            send_sem=send_sem.at[d, block, c],
            recv_sem=recv_sem.at[block, c],
            device_id={"node": there[d]},
            device_id_type=MESH,
        )

    def send(block, c, d, src):
        @pl.when(has[d])
        def _():
            copy(block, c, d, src).start()

    def arrived(block, c):
        copy(block, c, 0, out_ref.at[block, c]).wait_recv()

    def keep(c):
        return pltpu.make_async_copy(own.at[c], out_ref.at[me, c], local_sem.at[c])

    @pl.loop(0, pieces)
    def _(c):
        own[c] = jnp.where(act_ref[c] > 0, grad_ref[c], jnp.zeros_like(grad_ref[c]))
        for d in range(4):
            send(me, c, d, own.at[c])
        keep(c).start()

    own_in = pltpu.make_async_copy(in_ref, acts_ref.at[mine], in_local)
    own_in.start()
    for step in range(1, m):
        spread(step).start()

    @pl.loop(1, height)
    def _(t):
        @pl.loop(0, pieces)
        def _(c):
            for zz, onward in ((z + t, 0), (z - t, 1)):
                @pl.when((zz >= 0) & (zz < height))
                def _():
                    block = zz * width + x
                    arrived(block, c)
                    send(block, c, onward, out_ref.at[block, c])

                    @pl.when((zz != mate) | (c >= over))
                    def _():
                        for d in (2, 3):
                            send(block, c, d, out_ref.at[block, c])

            if over:
                @pl.when((t == 1) & (c < over))
                def _():
                    block = z * width + 1 - x
                    arrived(block, c)
                    for d in range(2):
                        @pl.when(z % 2 == 1 - d)
                        def _():
                            send(block, c, d, out_ref.at[block, c])

    @pl.loop(1, width)
    def _(s):
        @pl.loop(0, height)
        def _(zz):
            @pl.loop(0, pieces)
            def _(c):
                for xx, onward in ((x + s, 2), (x - s, 3)):
                    @pl.when((xx >= 0) & (xx < width) & ((zz != z) | (c >= over)))
                    def _():
                        block = zz * width + xx
                        arrived(block, c)
                        send(block, c, onward, out_ref.at[block, c])

    @pl.loop(0, n)
    def _(block):
        zz, xx = block // width, block % width

        @pl.loop(0, pieces)
        def _(c):
            direct = (zz != mate) | (c >= over)
            handed = (xx != x) & (zz == z) & (c < over)
            sent = (
                ((xx == x) & (zz >= z)) | (handed & (z % 2 == 1)),
                ((xx == x) & (zz <= z)) | (handed & (z % 2 == 0)),
                (xx >= x) & direct,
                (xx <= x) & direct,
            )
            for d in range(4):
                @pl.when(has[d] & sent[d])
                def _():
                    copy(block, c, d, out_ref.at[block, c]).wait_send()

    @pl.loop(0, pieces)
    def _(c):
        keep(c).wait()

    own_in.wait()
    for step in range(1, m):
        spread(step).wait()


def gather(n, m, grad, act, acts):
    feats, nodes = grad.shape
    width = 2 ** ((n.bit_length() - 1) // 2)
    rows = min(ROWS, feats)
    shape = (feats // rows, rows, nodes)
    pieces = shape[0]
    return pl.pallas_call(
        functools.partial(gather_kernel, n, m, width),
        out_shape=(
            jax.ShapeDtypeStruct((n, *shape), grad.dtype),
            jax.ShapeDtypeStruct((m, *acts.shape), acts.dtype),
        ),
        in_specs=[pl.BlockSpec(memory_space=pltpu.VMEM)] * 2 + [pl.BlockSpec(memory_space=pl.ANY)],
        out_specs=(pl.BlockSpec(memory_space=pl.ANY),) * 2,
        scratch_shapes=[
            pltpu.VMEM(shape, grad.dtype),
            pltpu.SemaphoreType.DMA((4, n, pieces)),
            pltpu.SemaphoreType.DMA((n, pieces)),
            pltpu.SemaphoreType.DMA((pieces,)),
            pltpu.SemaphoreType.DMA((m,)),
            pltpu.SemaphoreType.DMA((m,)),
            pltpu.SemaphoreType.DMA,
        ],
        compiler_params=pltpu.CompilerParams(
            collective_id=0, has_side_effects=True, vmem_limit_bytes=32 * 2**20
        ),
    )(grad.reshape(shape), act.reshape(shape), acts)


def sparse_kernel(index_ref, count_ref, whole_ref, tiles_ref, out_ref, held, sem):
    rows, slots, size, _ = tiles_ref.shape
    _, pieces, high, nodes = whole_ref.shape
    per_owner = nodes // size
    feats = pieces * high
    groups = slots // GROUP

    def copy(r, j):
        part = pl.ds(j * GROUP, GROUP)
        at = lax.rem(r, DEPTH)
        return pltpu.make_async_copy(tiles_ref.at[r, part], held.at[at, part], sem.at[at, j])

    def fetch(r):
        for j in range(groups):
            @pl.when(j * GROUP < count_ref[r])
            def _():
                copy(r, j).start()

    def picked(r, k, count):
        block = index_ref[r, k]
        owner = lax.div(block, per_owner)
        start = pl.multiple_of(lax.rem(block, per_owner) * size, size)
        got = whole_ref[owner, :, :, pl.ds(start, size)].reshape(feats, size)
        return jnp.where(k < count, got, jnp.zeros_like(got))

    @pl.loop(0, min(DEPTH - 1, rows))
    def _(r):
        fetch(r)

    @pl.loop(0, rows)
    def _(r):
        @pl.when(r + DEPTH - 1 < rows)
        def _():
            fetch(r + DEPTH - 1)

        count = count_ref[r]
        at = lax.rem(r, DEPTH)
        used = lax.div(count + GROUP - 1, GROUP)
        for b in range(1, groups + 1):
            @pl.when(used == b)
            def _():
                for j in range(b):
                    copy(r, j).wait()
                total = None
                for k in range(0, b * GROUP, 2):
                    left = jnp.concatenate(
                        [picked(r, k, count), picked(r, k + 1, count)], axis=1
                    )
                    right = jnp.concatenate([held[at, k], held[at, k + 1]], axis=1)
                    term = lax.dot_general(
                        left, right, (((1,), (1,)), ((), ())), preferred_element_type=jnp.float32
                    )
                    total = term if total is None else total + term
                share = rows // out_ref.shape[0]
                start = pl.multiple_of(lax.rem(r, share) * size, size)
                out_ref[lax.div(r, share), :, pl.ds(start, size)] = total.astype(out_ref.dtype)


def sparse(m, indices, counts, whole, tiles):
    rows, slots, size, _ = tiles.shape
    feats = whole.shape[1] * whole.shape[2]
    smem = pl.BlockSpec(memory_space=pltpu.SMEM)
    vmem = pl.BlockSpec(memory_space=pltpu.VMEM)
    return pl.pallas_call(
        sparse_kernel,
        out_shape=jax.ShapeDtypeStruct((m, feats, rows * size // m), whole.dtype),
        in_specs=[smem, smem, vmem, pl.BlockSpec(memory_space=pl.ANY)],
        out_specs=vmem,
        scratch_shapes=[
            pltpu.VMEM((DEPTH, slots, size, size), tiles.dtype),
            pltpu.SemaphoreType.DMA((DEPTH, slots // GROUP)),
        ],
        compiler_params=pltpu.CompilerParams(vmem_limit_bytes=48 * 2**20),
    )(indices, counts, whole, tiles)


def finish_kernel(
    n, m, scale, agg_ref, acts_ref, weight_ref, grad_ref, wgrad_ref,
    rows, parts, taken, node_part, agg_send, agg_recv, part_send, part_recv,
    sum_send, sum_recv, all_send, all_recv,
):
    node, feat = lax.axis_index("node"), lax.axis_index("feat")
    feats, share = agg_ref.shape[1:]
    high = parts.shape[1]

    barrier = pltpu.get_barrier_semaphore()
    for step in range(1, m):
        pl.semaphore_signal(
            barrier, inc=1, device_id={"feat": lax.rem(feat + step, m)}, device_id_type=MESH
        )

    @pl.loop(1, n)
    def _(step):
        pl.semaphore_signal(
            barrier, inc=1, device_id={"node": lax.rem(node + step, n)}, device_id_type=MESH
        )

    pl.semaphore_wait(barrier, m + n - 2)

    def agg_copy(step):
        to = lax.rem(feat + step, m)
        return pltpu.make_async_remote_copy(
            src_ref=agg_ref.at[to],
            dst_ref=rows.at[feat],
            send_sem=agg_send.at[step],
            recv_sem=agg_recv.at[step],
            device_id={"feat": to},
            device_id_type=MESH,
        )

    def part_copy(step):
        to = lax.rem(node + step, n)
        return pltpu.make_async_remote_copy(
            src_ref=parts.at[to],
            dst_ref=taken.at[node],
            send_sem=part_send.at[step],
            recv_sem=part_recv.at[step],
            device_id={"node": to},
            device_id_type=MESH,
        )

    def sum_copy(step):
        return pltpu.make_async_remote_copy(
            src_ref=node_part,
            dst_ref=wgrad_ref.at[feat, node],
            send_sem=sum_send.at[step],
            recv_sem=sum_recv.at[step],
            device_id={"node": lax.rem(node + step, n)},
            device_id_type=MESH,
        )

    def all_copy(step):
        return pltpu.make_async_remote_copy(
            src_ref=wgrad_ref.at[feat],
            dst_ref=wgrad_ref.at[feat],
            send_sem=all_send.at[step],
            recv_sem=all_recv.at[step],
            device_id={"feat": lax.rem(feat + step, m)},
            device_id_type=MESH,
        )

    for step in range(1, m):
        agg_copy(step).start()
    rows[feat] = agg_ref[feat]

    total = None
    for q in range(m):
        term = lax.dot_general(
            agg_ref[q], acts_ref[q], (((1,), (1,)), ((), ())), preferred_element_type=jnp.float32
        )
        total = term if total is None else total + term
    total = total * scale
    for i in range(n):
        parts[i] = total[i * high : (i + 1) * high]
    taken[node] = parts[node]

    @pl.loop(1, n)
    def _(step):
        part_copy(step).start()

    @pl.loop(1, n)
    def _(step):
        part_copy(step).wait()

    node_part[...] = jnp.sum(taken[...], axis=0)
    wgrad_ref[feat, node] = node_part[...]

    @pl.loop(1, n)
    def _(step):
        sum_copy(step).start()

    @pl.loop(1, n)
    def _(step):
        sum_copy(step).wait()

    for step in range(1, m):
        all_copy(step).start()
    for step in range(1, m):
        agg_copy(step).wait()

    wide = min(512, share)

    @pl.loop(0, share // wide)
    def _(i):
        at = pl.ds(pl.multiple_of(i * wide, wide), wide)
        right = rows[:, :, at].reshape(m * feats, wide)
        grad_ref[:, at] = jnp.dot(
            weight_ref[...], right, preferred_element_type=jnp.float32
        ).astype(grad_ref.dtype)

    for step in range(1, m):
        all_copy(step).wait()


def finish(n, m, scale, aggregated, acts, weight):
    _, feats, share = aggregated.shape
    high, wide = feats // n, acts.shape[1]
    dma = pltpu.SemaphoreType.DMA
    return pl.pallas_call(
        functools.partial(finish_kernel, n, m, scale),
        out_shape=(
            jax.ShapeDtypeStruct((weight.shape[0], share), aggregated.dtype),
            jax.ShapeDtypeStruct((m, n, high, wide), jnp.float32),
        ),
        in_specs=[pl.BlockSpec(memory_space=pltpu.VMEM)] * 3,
        out_specs=(pl.BlockSpec(memory_space=pltpu.VMEM),) * 2,
        scratch_shapes=[
            pltpu.VMEM((m, feats, share), aggregated.dtype),
            pltpu.VMEM((n, high, wide), jnp.float32),
            pltpu.VMEM((n, high, wide), jnp.float32),
            pltpu.VMEM((high, wide), jnp.float32),
            dma((m,)), dma((m,)), dma((n,)), dma((n,)), dma((n,)), dma((n,)), dma((m,)), dma((m,)),
        ],
        compiler_params=pltpu.CompilerParams(
            collective_id=1, has_side_effects=True, vmem_limit_bytes=48 * 2**20
        ),
    )(aggregated, acts, weight)


def per_device(nodes_n, feats_n, out_grad, pre_act, in_act, weight, tiles, indices, counts):
    whole, acts = gather(nodes_n, feats_n, out_grad, pre_act, in_act)
    aggregated = sparse(feats_n, indices, counts, whole, tiles)
    scale = float(nodes_n * out_grad.shape[1]) ** (-0.5)
    in_grad, turned = finish(nodes_n, feats_n, scale, aggregated, acts, weight)
    high, wide = weight.shape
    return in_grad, turned.reshape(wide, high).T


def solution(mesh):
    in_specs = (
        P("feat", "node"),
        P("feat", "node"),
        P(None, ("node", "feat")),
        P(),
        P("node", None, None, None),
        P("node", None),
        P("node"),
    )
    out_specs = (P(None, ("node", "feat")), P())
    return jax.shard_map(
        functools.partial(per_device, mesh.shape["node"], mesh.shape["feat"]),
        mesh=mesh,
        in_specs=in_specs,
        out_specs=out_specs,
        check_vma=False,
    )
```

time: 272 us -> 149 us (0.55)
  Pallas kernels: 0 us -> 137 us
  waiting for transfers between devices: 126 us -> 0 us
  blocking collectives: 40 us -> 0 us
  local copies, waits for them, and re-layouts: 51.8 us -> 12.1 us
  matrix products: 31.4 us -> 0 us
  between operations: 14.1 us -> 0.68 us
  other arithmetic: 4.82 us -> 0 us
  starting transfers between devices: 3.78 us -> 0 us
    pallas_call x0 -> x3, Pallas kernels: none -> 137 us  [the longest x1 94.2 us: gather(): pl.pallas_call(functools.partial(gather_kernel, n, m, width), out_shape=(...]
    all_gather x2 -> x0, waiting for transfers between devices: 125 us -> none  [the longest x1 125 us: per_device(): whole = lax.all_gather(grad_pre, 'node', axis=1, tiled=True)]
    gather x1 -> x0, local copies, waits for them, and re-layouts: 37.1 us -> none  [per_device(): picked = jnp.take(blocks, indices, axis=1)]
    psum x1 -> x0, blocking collectives: 34.6 us -> none  [per_device(): lax.psum(column_part.astype(jnp.bfloat16), 'node').astype(jnp.float32)]
    dot_general x3 -> x0, matrix products: 31.4 us -> none  [the longest x1 27.3 us: per_device(): jnp.einsum('frkc,rkic->fri', picked, tiles, preferred_element_type=jnp.fl...]
    unnamed x4 -> x16, local copies, waits for them, and re-layouts: 2.24 us -> 11.3 us
    reshape x1, local copies, waits for them, and re-layouts: 9.71 us -> 0.84 us  [per_device(): return (in_grad, turned.reshape(wide, high).T)]
    all_gather x1 -> x0, blocking collectives: 5.41 us -> none  [per_device(): lax.all_gather(column_part.astype(jnp.bfloat16), 'feat', axis=1, tiled=True)]
  transfers between devices with their start and end apart: 3 -> 0, of which waited for: 1 -> 0; matrix products, arithmetic and copies ran while one was open for 31% -> 0% of each run, Pallas kernels for 0% -> 0%
where the time goes in v1:
time: 149 us; the launch traced here: 150 us
  Pallas kernels  137 us (92%)
  local copies, waits for them, and re-layouts  12.1 us (8%)
    pallas_call x1, Pallas kernels, gather(): pl.pallas_call(functools.partial(gather_kernel, n, m, width), out_shape=(...  94.2 us
    pallas_call x1, Pallas kernels, sparse(): pl.pallas_call(sparse_kernel, out_shape=jax.ShapeDtypeStruct((m, feats, r...  23.8 us
    pallas_call x1, Pallas kernels, finish(): pl.pallas_call(functools.partial(finish_kernel, n, m, scale), out_shape=(...  18.8 us
    unnamed x16, local copies, waits for them, and re-layouts  11.3 us

profile of v1, /device:TPU:0, one launch (start us, length us, event | category | flops | bytes accessed | tf_op | source)
XLA Modules:
  0.0 149.5 jit_solution(13223099206235336518)
XLA Ops:
  0.6 0.8 copy.9.index_ref
  1.4 0.0 copy-start.2
  1.4 1.2 copy-done.2
  2.6 0.0 copy-start.3
  2.6 1.2 copy-done.3
  3.9 0.0 copy-start.4
  3.9 1.2 copy-done.4
  5.1 94.2 %shard_map.86 = (bf16[8,4,16,8192]{3,2,1,0:T(8,128)(2,1)S(1)}, bf16[4,256,2048]{2,1,0:T(8,128)(2,1)S(1)}) custom-call(bf16[4,16,8192]{2,1,0:T(8,128)(2,1)S(1)} %bitcast.4, bf16[4,16,8192]{2,1,0:T(8,128)(2,1)S(1)} %bitcast.5, bf16[256,2048]{1,0:T(8,128)(2,1)S(1)} %copy-done.4), custom_call_target="tpu_custom_call" | custom-call | tf_op jit(solution)/shard_map/pallas_call | solution.py:158
  99.3 0.0 copy-start
  99.3 3.2 %copy-done = bf16[8,4,16,8192]{3,2,1,0:T(8,128)(2,1)} copy-done((bf16[8,4,16,8192]{3,2,1,0:T(8,128)(2,1)}, bf16[8,4,16,8192]{3,2,1,0:T(8,128)(2,1)S(1)}, u32[]{:S(2)}) %copy-start) | copy-done | bytes 8388632
  102.5 0.0 copy-start.1
  102.5 2.0 %copy-done.1 = bf16[4,256,2048]{2,1,0:T(8,128)(2,1)} copy-done((bf16[4,256,2048]{2,1,0:T(8,128)(2,1)}, bf16[4,256,2048]{2,1,0:T(8,128)(2,1)S(1)}, u32[]{:S(2)}) %copy-start.1) | copy-done | bytes 4194328
  104.5 0.0 copy-start.6
  104.5 0.7 copy-done.6
  105.1 0.0 copy-start.5
  105.1 23.8 %shard_map.87.agg_ref = bf16[4,64,2048]{2,1,0:T(8,128)(2,1)S(1)} custom-call(s32[64,24]{1,0:T(8,128)S(1)} %copy.9.index_ref, s32[64]{0:T(128)S(1)} %copy-done.6, bf16[8,4,16,8192]{3,2,1,0:T(8,128)(2,1)} %copy-done, bf16[64,24,128,128]{3,2,1,0:T(8,128)(2,1)} %tiles_ref.1), custom_call_target="tpu_custom_call" | custom-call | tf_op jit(solution)/shard_map/pallas_call | solution.py:244
  128.9 0.0 copy-done.5
  128.9 18.8 %shard_map.88 = (bf16[256,2048]{1,0:T(8,128)(2,1)S(1)}, f32[4,8,8,256]{3,2,1,0:T(8,128)S(1)}) custom-call(bf16[4,64,2048]{2,1,0:T(8,128)(2,1)S(1)} %shard_map.87.agg_ref, bf16[4,256,2048]{2,1,0:T(8,128)(2,1)} %copy-done.1, bf16[256,256]{1,0:T(8,128)(2,1)S(1)} %copy-done.5), custom_call_target="tpu_custom_call" | custom-call | tf_op jit(solution)/shard_map/pallas_call | solution.py:379
  147.7 0.8 copy.10
  148.5 1.0 copy.12
Async XLA Ops:
  1.4 1.2 copy-start.2
  2.6 1.2 copy-start.3
  3.9 1.2 copy-start.4
  99.3 3.2 %copy-start = (bf16[8,4,16,8192]{3,2,1,0:T(8,128)(2,1)}, bf16[8,4,16,8192]{3,2,1,0:T(8,128)(2,1)S(1)}, u32[]{:S(2)}) copy-start(bf16[8,4,16,8192]{3,2,1,0:T(8,128)(2,1)S(1)} %get-tuple-element.6.whole_ref) | copy-start | bytes 25165828
  102.5 2.0 %copy-start.1 = (bf16[4,256,2048]{2,1,0:T(8,128)(2,1)}, bf16[4,256,2048]{2,1,0:T(8,128)(2,1)S(1)}, u32[]{:S(2)}) copy-start(bf16[4,256,2048]{2,1,0:T(8,128)(2,1)S(1)} %get-tuple-element.7.acts_ref) | copy-start | bytes 12582916
  104.5 0.7 copy-start.6
  105.1 23.8 %copy-start.5 = (bf16[256,256]{1,0:T(8,128)(2,1)S(1)}, bf16[256,256]{1,0:T(8,128)(2,1)}, u32[]{:S(2)}) copy-start(bf16[256,256]{1,0:T(8,128)(2,1)} %weight_ref.1) | copy-start | bytes 393220
